TPU v7x, 32 devices: a whole 2x2x4 slice. The times are simulated.
32 devices in a mesh: grp: 2 (over y), ex: 4 (over x, core), row: 4 (over z).
Axes of the slice: x: 2, y: 2, z: 4, core: 2. Of those that a mesh axis runs over, the one named last changes fastest.
Arguments:
- hidden: bfloat16 [16384, 28672], P(('grp', 'ex'), 'row'), parts along dimension 0, may hold values from -6 to 6
- out_grads: bfloat16 [16384, 8192], P(('grp', 'ex'), 'row'), parts along dimension 0, may hold values from -6 to 6
- proj_hidden: bfloat16 [28672, 512], P('row'), may hold values from -0.03125 to 0.03125
- proj_grads: bfloat16 [8192, 512], P('row'), may hold values from -0.0625 to 0.0625
- lengths: int32 [128], P('grp'), parts along dimension 0, may hold values from 1 to 512, 8192 in all
- owner_slots: int32 [128], P('grp'), parts along dimension 0, may hold values from 0 to 63, each once
Outputs:
- features: float32 [128, 512], P(('grp', 'ex')), parts along dimension 0
There are 2 independent parts, one for each index of `grp`. A program takes and returns all parts, laid end to end along the dimension named above; an argument that names none is the same for every part. Nothing has to cross between parts.
Inputs may be any that keep to these rules, and one draw needn't show every extreme that they name: `lengths`: they sum to 8192; some example has exactly 512 tokens. `owner_slots`: each of the 64 rows is named once.
All inputs are finite; a program needn't handle non-finite values.
Results may differ from a plain program's by a relative error of at most 0.0029.
Values may be sent and summed in bfloat16 or wider, within the bound.
A program may use at most 128 MiB of HBM per device.

v0:
```python
import jax
import jax.numpy as jnp
from jax import lax
from jax.sharding import PartitionSpec as P


def per_device(hidden, out_grads, proj_hidden, proj_grads, lengths, owner_slots):
    tok_count = hidden.shape[0]
    example_count = lengths.shape[0]
    shares = lax.psum_scatter(
        jnp.dot(out_grads, proj_grads, preferred_element_type=jnp.float32),
        "row",
        scatter_dimension=0,
        tiled=True,
    )
    shares_low = shares.astype(jnp.bfloat16)
    hid_part = jnp.dot(hidden, proj_hidden, preferred_element_type=jnp.float32)
    doc_ends = jnp.cumsum(lengths)
    doc_starts = doc_ends - lengths
    grad_proj = lax.all_gather(shares_low, "row", axis=0, tiled=True)
    product = hid_part * grad_proj.astype(jnp.float32)
    position = lax.axis_index("ex") * tok_count + jnp.arange(tok_count, dtype=jnp.int32)
    member = (
        (position[:, None] >= doc_starts[None, :]) & (position[:, None] < doc_ends[None, :])
    ).astype(jnp.float32)
    partial_value = jnp.dot(member.T, product, precision=lax.Precision.HIGHEST)
    partial_value = partial_value / jnp.sqrt(lengths.astype(jnp.float32))[:, None]
    slot_ids = jnp.arange(example_count, dtype=jnp.int32)
    placing = (slot_ids[:, None] == owner_slots[None, :]).astype(jnp.float32)
    arranged = jnp.dot(placing, partial_value, precision=lax.Precision.HIGHEST)
    per_owner = example_count // lax.axis_size("ex")
    summed = lax.psum(arranged, ("ex", "row"))
    return lax.dynamic_slice_in_dim(summed, lax.axis_index("ex") * per_owner, per_owner, 0)


def solution(mesh):
    placed = (
        P(("grp", "ex"), "row"),
        P(("grp", "ex"), "row"),
        P("row", None),
        P("row", None),
        P("grp"),
        P("grp"),
    )
    return jax.shard_map(
        per_device, mesh=mesh, in_specs=placed, out_specs=P(("grp", "ex"), None), check_vma=False
    )
```

profile of v0, /device:TPU:0, one launch (start us, length us, event | category | flops | bytes accessed | tf_op | source)
XLA Modules:
  0.0 245.0 jit_solution(9204776083419900372)
XLA Ops:
  6.5 0.0 copy-start
  6.5 0.0 reduce-scatter.2.cloned.1.call-start
  6.5 1.6 copy-done
  8.1 9.5 %fusion.15 = f32[2048,512]{1,0:T(8,128)} fusion(bf16[2048,2048]{1,0:T(8,128)(2,1)} %param.7, bf16[2048,512]{1,0:T(8,128)(2,1)S(1)} %copy-done), kind=kOutput, calls=%fused_computation.17 | convolution fusion | flops 4294967296 | bytes 14680064 | tf_op jit(solution)/shard_map/dot_general | solution.py:11
  17.7 0.0 copy-start.1
  17.7 0.0 reduce-scatter.2.cloned.1.call-update
  17.7 0.0 all-gather.2.cloned.1.call-start
  17.7 0.6 copy-done.1
  18.3 0.1 copy.8
  18.4 0.1 reduce-window.8
  18.5 0.1 reduce
  18.7 78.7 %reduce-scatter.2.cloned.1.call-done = f32[512,512]{1,0:T(8,128)} async-done(((f32[2048,512]{1,0:T(8,128)}), f32[512,512]{1,0:T(8,128)}) %reduce-scatter.2.cloned.1.call-update) | async-done | bytes 1048592 | tf_op jit(solution)/shard_map/reduce_scatter | solution.py:10
  97.3 2.1 convert_element_type.11
  99.4 0.0 all-gather.2.cloned.1.call-update
  99.4 0.0 all-reduce.2.cloned.1.call-start
  99.5 23.0 %fusion.14 = f32[2048,512]{1,0:T(8,128)} fusion(bf16[2048,7168]{1,0:T(8,128)(2,1)} %param.6, bf16[7168,512]{1,0:T(8,128)(2,1)} %param.8), kind=kOutput, calls=%fused_computation.16 | convolution fusion | flops 15032385536 | bytes 40894464 | tf_op jit(solution)/shard_map/dot_general | solution.py:17
  122.4 0.0 copy-start.2
  122.4 23.5 %all-gather.2.cloned.1.call-done = bf16[2048,512]{1,0:T(8,128)(2,1)} async-done(((bf16[512,512]{1,0:T(8,128)(2,1)}), bf16[2048,512]{1,0:T(8,128)(2,1)}) %all-gather.2.cloned.1.call-update) | async-done | bytes 2097168 | tf_op jit(solution)/shard_map/all_gather | solution.py:20
  146.0 4.3 %fusion.3 = f32[64,512]{1,0:T(8,128)S(1)} fusion(f32[2048,512]{1,0:T(8,128)} %fusion.14, bf16[2048,512]{1,0:T(8,128)(2,1)} %all-gather.2.cloned.1.call-done, s32[64]{0:T(128)S(1)} %reduce, s32[64]{0:T(128)S(1)} %sub.3, s32[2048]{0:T(1024)S(1)} %iota_add_fusion, f32[64]{0:T(128)S(1)} %convert_sqrt_fusion), kind=kOutput, calls=%fused_computation.3 | convolution fusion | flops 807829504 | bytes 6431488 | tf_op jit(solution)/shard_map/dot_general | solution.py:26
  150.3 0.0 copy-done.2
  150.3 0.9 fusion.12
  151.1 0.0 all-reduce.2.cloned.1.call-update
  151.2 85.9 %all-reduce.2.cloned.1.call-done = f32[64,512]{1,0:T(8,128)} async-done(((f32[64,512]{1,0:T(8,128)}), f32[64,512]{1,0:T(8,128)}) %all-reduce.2.cloned.1.call-update) | async-done | bytes 131088 | tf_op jit(solution)/shard_map/psum | solution.py:32
  237.1 1.4 constant_dynamic-slice_fusion
  (3 shorter events, 0.0 us)
Async XLA Ops:
  6.5 1.6 copy-start
  6.5 90.8 %reduce-scatter.2.cloned.1.call-start = ((), (), s32[]{:S(2)}) async-start(), calls=%async_computation.1 | async-start | bytes 5242880 | tf_op jit(solution)/shard_map/reduce_scatter | solution.py:10
  17.7 0.7 copy-start.1
  17.7 128.3 %all-gather.2.cloned.1.call-start = ((), (), s32[]{:S(2)}) async-start(), calls=%async_computation.2 | async-start | bytes 2621440 | tf_op jit(solution)/shard_map/all_gather | solution.py:20
  99.4 137.6 %all-reduce.2.cloned.1.call-start = ((), (), s32[]{:S(2)}) async-start(), calls=%async_computation.3 | async-start | bytes 262144 | tf_op jit(solution)/shard_map/psum | solution.py:32
  122.4 27.8 %copy-start.2 = (s32[64]{0:T(128)S(1)}, s32[64]{0:T(128)}, u32[]{:S(2)}) copy-start(s32[64]{0:T(128)} %param.11) | copy-start | bytes 772
Sparse Core Ops, SparseCore 0:
  17.8 79.4 reduce-scatter.1
  99.6 46.3 all-gather.1
  151.3 85.7 all-reduce.1
where the time goes:
time: 246 us; the launch traced here: 245 us
  waiting for transfers between devices  188 us (76%)
  matrix products  37.6 us (15%)
  between operations  13.2 us (5%)
  local copies, waits for them, and re-layouts  3.64 us (1%)
    psum x1, waiting for transfers between devices, per_device(): summed = lax.psum(arranged, ('ex', 'row'))  85.9 us
    reduce_scatter x1, waiting for transfers between devices, per_device(): lax.psum_scatter(jnp.dot(out_grads, proj_grads, preferred_element_type=jn...  78.7 us
    all_gather x1, waiting for transfers between devices, per_device(): grad_proj = lax.all_gather(shares_low, 'row', axis=0, tiled=True)  23.5 us
    dot_general x1, matrix products, per_device(): hid_part = jnp.dot(hidden, proj_hidden, preferred_element_type=jnp.float32)  23 us
    dot_general x1, matrix products, per_device(): jnp.dot(out_grads, proj_grads, preferred_element_type=jnp.float32)  9.53 us
  transfers between devices with their start and end apart: 3, of which 3 were waited for; matrix products, arithmetic and copies ran while one was open for 9% of the time, Pallas kernels for 0%

commit v1 on v0

v1 whole, which is shorter than its diff:
```python
import functools

import jax
import jax.numpy as jnp
from jax import lax
from jax.experimental import pallas as pl
from jax.experimental.pallas import tpu as pltpu
from jax.sharding import PartitionSpec as P

MESH = pl.DeviceIdType.MESH
TILE = 256
CHUNK = 64
PER = TILE // CHUNK
RING = 8
LEAD = 4
PEER_LAG = 2
LAG = 4


def sums_kernel(
    ex_count, len_ref, own_ref, og_hbm, pg_hbm, hid_hbm, ph_hbm, out_ref,
    og, pg, ph, hid, grad, hidp, near_out, peer_out, near_in, peer_in,
    lo, hi, acc, block, got_ex, got_row,
    pg_sem, og_sem, ph_sem, hid_sem,
    near_send, near_recv, peer_send, peer_recv, ex_send, ex_recv, row_send, row_recv,
):
    ex = lax.axis_index("ex")
    row = lax.axis_index("row")
    tokens = og_hbm.shape[0]
    tiles = tokens // TILE
    chunks = tokens // CHUNK
    examples = len_ref.shape[1]
    per_owner = examples // ex_count
    depth = ph_hbm.shape[0] // PER
    near = row + 1 - 2 * (row % 2)
    peer = 3 - row
    is_mid = (row == 1) | (row == 2)
    is_end = (row == 0) | (row == 3)

    def load_og(i):
        return pltpu.make_async_copy(
            og_hbm.at[pl.ds(pl.multiple_of(i * TILE, TILE), TILE)], og.at[i], og_sem.at[i]
        )

    def load_ph(k):
        return pltpu.make_async_copy(
            ph_hbm.at[pl.ds(pl.multiple_of(k * depth, depth), depth)], ph.at[k], ph_sem.at[k]
        )

    def load_hid(s):
        i, k = s // PER, s % PER
        return pltpu.make_async_copy(
            hid_hbm.at[
                pl.ds(pl.multiple_of(i * TILE, TILE), TILE),
                pl.ds(pl.multiple_of(k * depth, 128), depth),
            ],
            hid.at[s % RING],
            hid_sem.at[s % RING],
        )

    def near_copy(c):
        return pltpu.make_async_remote_copy(
            src_ref=near_out.at[c], dst_ref=near_in.at[c],
            send_sem=near_send.at[c], recv_sem=near_recv.at[c],
            device_id={"row": near}, device_id_type=MESH,
        )

    def peer_copy(c):
        return pltpu.make_async_remote_copy(
            src_ref=peer_out.at[c], dst_ref=peer_in.at[c],
            send_sem=peer_send.at[c], recv_sem=peer_recv.at[c],
            device_id={"row": peer}, device_id_type=MESH,
        )

    pg_copy = pltpu.make_async_copy(pg_hbm, pg, pg_sem)
    pg_copy.start()
    load_og(0).start()
    load_og(1).start()
    barrier = pltpu.get_barrier_semaphore()
    for d in range(1, ex_count):
        pl.semaphore_signal(barrier, inc=1, device_id={"ex": (ex + d) % ex_count}, device_id_type=MESH)
    for d in range(1, 4):
        pl.semaphore_signal(barrier, inc=1, device_id={"row": (row + d) % 4}, device_id_type=MESH)
    for k in range(PER):
        load_ph(k).start()
        load_hid(k).start()
    for i in range(2, tiles):
        load_og(i).start()
    for s in range(PER, RING):
        load_hid(s).start()

    length = len_ref[...].astype(jnp.float32)
    r = lax.broadcasted_iota(jnp.int32, (examples, examples), 0)
    c = lax.broadcasted_iota(jnp.int32, (examples, examples), 1)
    ends = jnp.sum(jnp.where(c <= r, length, 0.0), axis=1, keepdims=True)
    ends = jnp.sum(jnp.where(r == c, ends, 0.0), axis=0, keepdims=True)
    starts = ends - length
    mine = own_ref[...] == r
    hi[...] = jnp.broadcast_to(
        jnp.sum(jnp.where(mine, ends, 0.0), axis=1, keepdims=True), hi.shape
    )
    lo[...] = jnp.broadcast_to(
        jnp.sum(jnp.where(mine, starts, 0.0), axis=1, keepdims=True), lo.shape
    )
    acc[...] = jnp.zeros_like(acc)

    def grad_tile(i):
        load_og(i).wait()
        g = jnp.dot(og[i], pg[...], preferred_element_type=jnp.float32)
        g = g.reshape(PER, CHUNK, g.shape[-1])
        at = pl.ds(pl.multiple_of(i * PER, PER), PER)
        grad[at] = g

        @pl.when(is_end)
        def _():
            near_out[at] = g.astype(jnp.bfloat16)

    pg_copy.wait()
    grad_tile(0)
    pl.semaphore_wait(barrier, ex_count - 1 + 3)

    @pl.when(is_end)
    def _():
        for m in range(LEAD):
            near_copy(m).start()

    grad_tile(1)

    def add_up(m, total):
        product = total * hidp[m]
        high = product.astype(jnp.bfloat16)
        low = (product - high.astype(jnp.float32)).astype(jnp.bfloat16)
        position = (
            ex * tokens + m * CHUNK + lax.broadcasted_iota(jnp.int32, (examples, CHUNK), 1)
        ).astype(jnp.float32)
        member = jnp.where(
            (position >= lo[:, :CHUNK]) & (position < hi[:, :CHUNK]), 1.0, 0.0
        ).astype(jnp.bfloat16)
        acc[...] += jnp.dot(member, high, preferred_element_type=jnp.float32) + jnp.dot(
            member, low, preferred_element_type=jnp.float32
        )

    def step(s, carry):
        i, k = s // PER, s % PER

        @pl.when(s < chunks)
        def _():
            load_hid(s).wait()

            @pl.when(i == 0)
            def _():
                load_ph(k).wait()

            h = jnp.dot(hid[s % RING], ph[k], preferred_element_type=jnp.float32)
            h = h.reshape(PER, CHUNK, h.shape[-1])
            at = pl.ds(pl.multiple_of(i * PER, PER), PER)

            @pl.when(k == 0)
            def _():
                hidp[at] = h

            @pl.when(k > 0)
            def _():
                hidp[at] += h

            @pl.when(s + RING < chunks)
            def _():
                load_hid(s + RING).start()

        @pl.when((k == 0) & (i + 2 < tiles))
        def _():
            grad_tile(i + 2)

        @pl.when(is_end & (s + LEAD < chunks))
        def _():
            near_copy(s + LEAD).start()

        @pl.when(is_mid & (s < chunks))
        def _():
            near_copy(s).wait_recv()
            peer_out[s] = (near_in[s].astype(jnp.float32) + grad[s]).astype(jnp.bfloat16)
            peer_copy(s).start()

        @pl.when(is_mid & (s >= PEER_LAG) & (s < chunks + PEER_LAG))
        def _():
            m = s - PEER_LAG
            peer_copy(m).wait_recv()
            near_out[m] = (peer_in[m].astype(jnp.float32) + grad[m]).astype(jnp.bfloat16)
            near_copy(m).start()

        @pl.when(is_end & (s >= LAG))
        def _():
            m = s - LAG
            near_copy(m).wait_recv()
            add_up(m, grad[m] + near_in[m].astype(jnp.float32))

        @pl.when(is_mid & (s >= LAG))
        def _():
            m = s - LAG
            add_up(
                m, grad[m] + near_in[m].astype(jnp.float32) + peer_in[m].astype(jnp.float32)
            )

        return carry

    lax.fori_loop(0, chunks + LAG, step, 0)

    acc[...] = acc[...] / jnp.sqrt(hi[:, :1] - lo[:, :1])

    def ex_copy(d):
        to = (ex + d) % ex_count
        return pltpu.make_async_remote_copy(
            src_ref=acc.at[pl.ds(pl.multiple_of(to * per_owner, per_owner), per_owner)],
            dst_ref=got_ex.at[d - 1],
            send_sem=ex_send.at[d - 1], recv_sem=ex_recv.at[d - 1],
            device_id={"ex": to}, device_id_type=MESH,
        )

    for d in range(1, ex_count):
        ex_copy(d).start()
    total = acc[pl.ds(pl.multiple_of(ex * per_owner, per_owner), per_owner)]
    for d in range(1, ex_count):
        ex_copy(d).wait_recv()
        total = total + got_ex[d - 1]
    block[...] = total

    def row_copy(d):
        return pltpu.make_async_remote_copy(
            src_ref=block, dst_ref=got_row.at[row],
            send_sem=row_send.at[d - 1], recv_sem=row_recv.at[row],
            device_id={"row": (row + d) % 4}, device_id_type=MESH,
        )

    for d in range(1, 4):
        row_copy(d).start()
    for d in range(1, 4):
        source = (row + d) % 4
        pltpu.make_async_remote_copy(
            src_ref=block, dst_ref=got_row.at[source],
            send_sem=row_send.at[d - 1], recv_sem=row_recv.at[source],
            device_id={"row": source}, device_id_type=MESH,
        ).wait_recv()
    got_row[row] = total
    out_ref[...] = (got_row[0] + got_row[1]) + (got_row[2] + got_row[3])

    for d in range(1, ex_count):
        ex_copy(d).wait_send()
    for d in range(1, 4):
        row_copy(d).wait_send()

    def drain(m, carry):
        near_copy(m).wait_send()

        @pl.when(is_mid)
        def _():
            peer_copy(m).wait_send()

        return carry

    lax.fori_loop(0, chunks, drain, 0)


def with_kernel(ex_count, hidden, out_grads, proj_hidden, proj_grads, lengths, owner_slots):
    tokens, units = hidden.shape
    features = out_grads.shape[1]
    k_dim = proj_hidden.shape[1]
    examples = lengths.shape[0]
    per_owner = examples // ex_count
    tiles, chunks = tokens // TILE, tokens // CHUNK
    bf16, f32 = jnp.bfloat16, jnp.float32
    dma = pltpu.SemaphoreType.DMA
    messages = pltpu.VMEM((chunks, CHUNK, k_dim), bf16)
    return pl.pallas_call(
        functools.partial(sums_kernel, ex_count),
        out_shape=jax.ShapeDtypeStruct((per_owner, k_dim), f32),
        in_specs=[pl.BlockSpec(memory_space=pltpu.VMEM)] * 2
        + [pl.BlockSpec(memory_space=pl.ANY)] * 4,
        out_specs=pl.BlockSpec(memory_space=pltpu.VMEM),
        scratch_shapes=[
            pltpu.VMEM((tiles, TILE, features), bf16),
            pltpu.VMEM((features, k_dim), bf16),
            pltpu.VMEM((PER, units // PER, k_dim), bf16),
            pltpu.VMEM((RING, TILE, units // PER), bf16),
            pltpu.VMEM((chunks, CHUNK, k_dim), f32),
            pltpu.VMEM((chunks, CHUNK, k_dim), f32),
            messages, messages, messages, messages,
            pltpu.VMEM((examples, 128), f32),
            pltpu.VMEM((examples, 128), f32),
            pltpu.VMEM((examples, k_dim), f32),
            pltpu.VMEM((per_owner, k_dim), f32),
            pltpu.VMEM((ex_count - 1, per_owner, k_dim), f32),
            pltpu.VMEM((4, per_owner, k_dim), f32),
            dma, dma((tiles,)), dma((PER,)), dma((RING,)),
            dma((chunks,)), dma((chunks,)), dma((chunks,)), dma((chunks,)),
            dma((ex_count - 1,)), dma((ex_count - 1,)), dma((3,)), dma((4,)),
        ],
        compiler_params=pltpu.CompilerParams(
            collective_id=0, has_side_effects=True, vmem_limit_bytes=56 * 2**20
        ),
    )(lengths[None, :], owner_slots[None, :], out_grads, proj_grads, hidden, proj_hidden)


def with_collectives(hidden, out_grads, proj_hidden, proj_grads, lengths, owner_slots):
    tok_count = hidden.shape[0]
    example_count = lengths.shape[0]
    shares = lax.psum_scatter(
        jnp.dot(out_grads, proj_grads, preferred_element_type=jnp.float32),
        "row",
        scatter_dimension=0,
        tiled=True,
    )
    shares_low = shares.astype(jnp.bfloat16)
    hid_part = jnp.dot(hidden, proj_hidden, preferred_element_type=jnp.float32)
    doc_ends = jnp.cumsum(lengths)
    doc_starts = doc_ends - lengths
    grad_proj = lax.all_gather(shares_low, "row", axis=0, tiled=True)
    product = hid_part * grad_proj.astype(jnp.float32)
    position = lax.axis_index("ex") * tok_count + jnp.arange(tok_count, dtype=jnp.int32)
    slot_ids = jnp.arange(example_count, dtype=jnp.int32)
    placing = slot_ids[:, None] == owner_slots[None, :]
    start, end = (
        jnp.sum(jnp.where(placing, edge[None, :], 0), axis=1) for edge in (doc_starts, doc_ends)
    )
    member = (
        (position[None, :] >= start[:, None]) & (position[None, :] < end[:, None])
    ).astype(jnp.float32)
    arranged = jnp.dot(member, product, precision=lax.Precision.HIGHEST)
    arranged = arranged / jnp.sqrt((end - start).astype(jnp.float32))[:, None]
    per_owner = example_count // lax.axis_size("ex")
    summed = lax.psum(arranged, ("ex", "row"))
    return lax.dynamic_slice_in_dim(summed, lax.axis_index("ex") * per_owner, per_owner, 0)


def solution(mesh):
    sizes = dict(mesh.shape)
    if sizes["row"] == 4:
        body = functools.partial(with_kernel, sizes["ex"])
    else:
        body = with_collectives
    placed = (
        P(("grp", "ex"), "row"),
        P(("grp", "ex"), "row"),
        P("row", None),
        P("row", None),
        P("grp"),
        P("grp"),
    )
    return jax.shard_map(
        body, mesh=mesh, in_specs=placed, out_specs=P(("grp", "ex"), None), check_vma=False
    )
```

time: 246 us -> 77.4 us (0.31)
  waiting for transfers between devices: 188 us -> 0 us
  Pallas kernels: 0 us -> 75.8 us
  matrix products: 37.6 us -> 0 us
  between operations: 13.2 us -> 0.01 us
    psum x1 -> x0, waiting for transfers between devices: 85.9 us -> none  [per_device(): summed = lax.psum(arranged, ('ex', 'row'))]
    reduce_scatter x1 -> x0, waiting for transfers between devices: 78.7 us -> none  [per_device(): lax.psum_scatter(jnp.dot(out_grads, proj_grads, preferred_element_type=jn...]
    pallas_call x0 -> x1, Pallas kernels: none -> 75.8 us  [with_kernel(): pl.pallas_call(functools.partial(sums_kernel, ex_count), out_shape=jax.Sh...]
    dot_general x4 -> x0, matrix products: 37.6 us -> none  [the longest x1 23 us: per_device(): hid_part = jnp.dot(hidden, proj_hidden, preferred_element_type=jnp.float32)]
    all_gather x1 -> x0, waiting for transfers between devices: 23.5 us -> none  [per_device(): grad_proj = lax.all_gather(shares_low, 'row', axis=0, tiled=True)]
  transfers between devices with their start and end apart: 3 -> 0, of which waited for: 3 -> 0; matrix products, arithmetic and copies ran while one was open for 9% -> 0% of each run, Pallas kernels for 0% -> 0%
where the time goes in v1:
time: 77.4 us; the launch traced here: 77.2 us
  Pallas kernels  75.8 us (98%)
  local copies, waits for them, and re-layouts  1.38 us (2%)
    pallas_call x1, Pallas kernels, with_kernel(): pl.pallas_call(functools.partial(sums_kernel, ex_count), out_shape=jax.Sh...  75.8 us

profile of v1, /device:TPU:0, one launch (start us, length us, event | category | flops | bytes accessed | tf_op | source)
XLA Modules:
  0.0 77.2 jit_solution(17077661333995365176)
XLA Ops:
  0.0 75.8 %shard_map.64 = f32[16,512]{1,0:T(8,128)} custom-call(s32[1,64]{1,0:T(1,128)} %bitcast.2, s32[1,64]{1,0:T(1,128)} %bitcast.3, bf16[2048,2048]{1,0:T(8,128)(2,1)} %og_hbm.1, bf16[2048,512]{1,0:T(8,128)(2,1)} %pg_hbm.1, bf16[2048,7168]{1,0:T(8,128)(2,1)} %hid_hbm.1, bf16[7168,512]{1,0:T(8,128)(2,1)} %ph_hbm.1), custom_call_target="tpu_custom_call" | custom-call | tf_op jit(solution)/shard_map/pallas_call | solution.py:273
  75.8 1.4 %copy.8 = f32[16,512]{1,0:T(8,128)} copy(f32[16,512]{1,0:T(8,128)} %shard_map.64) | data formatting | bytes 65536

commit v2 on v1

--- a/solution.py
+++ b/solution.py
@@ -13,14 +13,15 @@
 PER = TILE // CHUNK
 RING = 8
 LEAD = 4
-PEER_LAG = 2
-LAG = 4
+PEER_LAG = 3
+HALVES = 1
+LAG = 6
 
 
 def sums_kernel(
     ex_count, len_ref, own_ref, og_hbm, pg_hbm, hid_hbm, ph_hbm, out_ref,
     og, pg, ph, hid, grad, hidp, near_out, peer_out, near_in, peer_in,
-    lo, hi, acc, block, got_ex, got_row,
+    lo, hi, acc, got_ex, got_row,
     pg_sem, og_sem, ph_sem, hid_sem,
     near_send, near_recv, peer_send, peer_recv, ex_send, ex_recv, row_send, row_recv,
 ):
@@ -28,6 +29,7 @@
     row = lax.axis_index("row")
     tokens = og_hbm.shape[0]
     tiles = tokens // TILE
+    width = og_hbm.shape[1] // PER
     chunks = tokens // CHUNK
     examples = len_ref.shape[1]
     per_owner = examples // ex_count
@@ -84,7 +86,9 @@
     for k in range(PER):
         load_ph(k).start()
         load_hid(k).start()
-    for i in range(2, tiles):
+        if k == 1:
+            load_og(2).start()
+    for i in range(3, tiles):
         load_og(i).start()
     for s in range(PER, RING):
         load_hid(s).start()
@@ -140,40 +144,52 @@
             member, low, preferred_element_type=jnp.float32
         )
 
+    def grad_piece(i, k):
+        at = pl.ds(pl.multiple_of(i * PER, PER), PER)
+        part = pl.ds(pl.multiple_of(k * width, 128), width)
+        g = jnp.dot(
+            og.at[i][:, part],
+            pg[pl.ds(pl.multiple_of(k * width, width), width)],
+            preferred_element_type=jnp.float32,
+        ).reshape(PER, CHUNK, pg.shape[-1])
+
+        @pl.when(k == 0)
+        def _():
+            grad[at] = g
+
+        @pl.when(k > 0)
+        def _():
+            grad[at] += g
+
+        @pl.when(is_end & (k == PER - 1))
+        def _():
+            near_out[at] = grad[at].astype(jnp.bfloat16)
+
+    def hidden_piece(s, i, k):
+        load_hid(s).wait()
+
+        @pl.when(i == 0)
+        def _():
+            load_ph(k).wait()
+
+        h = jnp.dot(hid[s % RING], ph[k], preferred_element_type=jnp.float32)
+        h = h.reshape(PER, CHUNK, h.shape[-1])
+        at = pl.ds(pl.multiple_of(i * PER, PER), PER)
+
+        @pl.when(k == 0)
+        def _():
+            hidp[at] = h
+
+        @pl.when(k > 0)
+        def _():
+            hidp[at] += h
+
+        @pl.when(s + RING < chunks)
+        def _():
+            load_hid(s + RING).start()
+
     def step(s, carry):
         i, k = s // PER, s % PER
-
-        @pl.when(s < chunks)
-        def _():
-            load_hid(s).wait()
-
-            @pl.when(i == 0)
-            def _():
-                load_ph(k).wait()
-
-            h = jnp.dot(hid[s % RING], ph[k], preferred_element_type=jnp.float32)
-            h = h.reshape(PER, CHUNK, h.shape[-1])
-            at = pl.ds(pl.multiple_of(i * PER, PER), PER)
-
-            @pl.when(k == 0)
-            def _():
-                hidp[at] = h
-
-            @pl.when(k > 0)
-            def _():
-                hidp[at] += h
-
-            @pl.when(s + RING < chunks)
-            def _():
-                load_hid(s + RING).start()
-
-        @pl.when((k == 0) & (i + 2 < tiles))
-        def _():
-            grad_tile(i + 2)
-
-        @pl.when(is_end & (s + LEAD < chunks))
-        def _():
-            near_copy(s + LEAD).start()
 
         @pl.when(is_mid & (s < chunks))
         def _():
@@ -188,6 +204,22 @@
             near_out[m] = (peer_in[m].astype(jnp.float32) + grad[m]).astype(jnp.bfloat16)
             near_copy(m).start()
 
+        @pl.when(is_end & (s + LEAD < chunks))
+        def _():
+            near_copy(s + LEAD).start()
+
+        @pl.when(s < chunks)
+        def _():
+            hidden_piece(s, i, k)
+
+        @pl.when(i + 2 < tiles)
+        def _():
+            @pl.when(k == 0)
+            def _():
+                load_og(i + 2).wait()
+
+            grad_piece(i + 2, k)
+
         @pl.when(is_end & (s >= LAG))
         def _():
             m = s - LAG
@@ -206,47 +238,54 @@
     lax.fori_loop(0, chunks + LAG, step, 0)
 
     acc[...] = acc[...] / jnp.sqrt(hi[:, :1] - lo[:, :1])
-
-    def ex_copy(d):
+    half = acc.shape[1] // HALVES
+
+    def ex_copy(d, q):
         to = (ex + d) % ex_count
         return pltpu.make_async_remote_copy(
-            src_ref=acc.at[pl.ds(pl.multiple_of(to * per_owner, per_owner), per_owner)],
-            dst_ref=got_ex.at[d - 1],
-            send_sem=ex_send.at[d - 1], recv_sem=ex_recv.at[d - 1],
+            src_ref=acc.at[
+                pl.ds(pl.multiple_of(to * per_owner, per_owner), per_owner),
+                pl.ds(q * half, half),
+            ],
+            dst_ref=got_ex.at[d - 1, :, pl.ds(q * half, half)],
+            send_sem=ex_send.at[d - 1, q], recv_sem=ex_recv.at[d - 1, q],
             device_id={"ex": to}, device_id_type=MESH,
         )
 
-    for d in range(1, ex_count):
-        ex_copy(d).start()
-    total = acc[pl.ds(pl.multiple_of(ex * per_owner, per_owner), per_owner)]
-    for d in range(1, ex_count):
-        ex_copy(d).wait_recv()
-        total = total + got_ex[d - 1]
-    block[...] = total
-
-    def row_copy(d):
+    def row_copy(d, q, source):
         return pltpu.make_async_remote_copy(
-            src_ref=block, dst_ref=got_row.at[row],
-            send_sem=row_send.at[d - 1], recv_sem=row_recv.at[row],
+            src_ref=got_row.at[row, :, pl.ds(q * half, half)],
+            dst_ref=got_row.at[source, :, pl.ds(q * half, half)],
+            send_sem=row_send.at[d - 1, q], recv_sem=row_recv.at[source, q],
             device_id={"row": (row + d) % 4}, device_id_type=MESH,
         )
 
-    for d in range(1, 4):
-        row_copy(d).start()
-    for d in range(1, 4):
-        source = (row + d) % 4
-        pltpu.make_async_remote_copy(
-            src_ref=block, dst_ref=got_row.at[source],
-            send_sem=row_send.at[d - 1], recv_sem=row_recv.at[source],
-            device_id={"row": source}, device_id_type=MESH,
-        ).wait_recv()
-    got_row[row] = total
-    out_ref[...] = (got_row[0] + got_row[1]) + (got_row[2] + got_row[3])
-
-    for d in range(1, ex_count):
-        ex_copy(d).wait_send()
-    for d in range(1, 4):
-        row_copy(d).wait_send()
+    for q in range(HALVES):
+        for d in range(1, ex_count):
+            ex_copy(d, q).start()
+    own_rows = pl.ds(pl.multiple_of(ex * per_owner, per_owner), per_owner)
+    for q in range(HALVES):
+        at = pl.ds(q * half, half)
+        total = acc[own_rows, at]
+        for d in range(1, ex_count):
+            ex_copy(d, q).wait_recv()
+            total = total + got_ex[d - 1, :, at]
+        got_row[row, :, at] = total
+        for d in range(1, 4):
+            row_copy(d, q, row).start()
+    for q in range(HALVES):
+        at = pl.ds(q * half, half)
+        for d in range(1, 4):
+            row_copy(d, q, (row + d) % 4).wait_recv()
+        out_ref[:, at] = (got_row[0, :, at] + got_row[1, :, at]) + (
+            got_row[2, :, at] + got_row[3, :, at]
+        )
+
+    for q in range(HALVES):
+        for d in range(1, ex_count):
+            ex_copy(d, q).wait_send()
+        for d in range(1, 4):
+            row_copy(d, q, row).wait_send()
 
     def drain(m, carry):
         near_copy(m).wait_send()
@@ -287,12 +326,11 @@
             pltpu.VMEM((examples, 128), f32),
             pltpu.VMEM((examples, 128), f32),
             pltpu.VMEM((examples, k_dim), f32),
-            pltpu.VMEM((per_owner, k_dim), f32),
             pltpu.VMEM((ex_count - 1, per_owner, k_dim), f32),
             pltpu.VMEM((4, per_owner, k_dim), f32),
             dma, dma((tiles,)), dma((PER,)), dma((RING,)),
             dma((chunks,)), dma((chunks,)), dma((chunks,)), dma((chunks,)),
-            dma((ex_count - 1,)), dma((ex_count - 1,)), dma((3,)), dma((4,)),
+            dma((ex_count - 1, HALVES)), dma((ex_count - 1, HALVES)), dma((3, HALVES)), dma((4, HALVES)),
         ],
         compiler_params=pltpu.CompilerParams(
             collective_id=0, has_side_effects=True, vmem_limit_bytes=56 * 2**20

time: 77.4 us -> 72.4 us (0.935)
  Pallas kernels: 75.8 us -> 70.8 us
    pallas_call x1, Pallas kernels: 75.8 us -> 70.8 us  [with_kernel(): pl.pallas_call(functools.partial(sums_kernel, ex_count), out_shape=jax.Sh...]
where the time goes in v2:
time: 72.4 us; the launch traced here: 72.2 us
  Pallas kernels  70.8 us (98%)
  local copies, waits for them, and re-layouts  1.38 us (2%)
    pallas_call x1, Pallas kernels, with_kernel(): pl.pallas_call(functools.partial(sums_kernel, ex_count), out_shape=jax.Sh...  70.8 us

profile of v2, /device:TPU:0, one launch (start us, length us, event | category | flops | bytes accessed | tf_op | source)
XLA Modules:
  0.0 72.2 jit_solution(1125418469454261677)
XLA Ops:
  0.0 70.8 %shard_map.64 = f32[16,512]{1,0:T(8,128)} custom-call(s32[1,64]{1,0:T(1,128)} %bitcast.2, s32[1,64]{1,0:T(1,128)} %bitcast.3, bf16[2048,2048]{1,0:T(8,128)(2,1)} %og_hbm.1, bf16[2048,512]{1,0:T(8,128)(2,1)} %pg_hbm.1, bf16[2048,7168]{1,0:T(8,128)(2,1)} %hid_hbm.1, bf16[7168,512]{1,0:T(8,128)(2,1)} %ph_hbm.1), custom_call_target="tpu_custom_call" | custom-call | tf_op jit(solution)/shard_map/pallas_call | solution.py:312
  70.9 1.4 %copy.8 = f32[16,512]{1,0:T(8,128)} copy(f32[16,512]{1,0:T(8,128)} %shard_map.64) | data formatting | bytes 65536
